TPU v7x, 768 devices: a whole 4x8x12 slice. The times are simulated.
768 devices in a mesh: dp: 32 (over y, x), row: 4 (over z_lo), col: 6 (over z_hi, core).
Axes of the slice: x: 4, y: 8, z: 12 (z_hi: 3, z_lo: 4; z = z_hi * 4 + z_lo), core: 2. Of those that a mesh axis runs over, the one named last changes fastest.
Arguments:
- tokens_in: bfloat16 [4608, 6144], P(('dp', 'col'), 'row'), may hold values from -6 to 6
- slot_values: bfloat16 [2048, 24576], P('row', 'col'), may hold values from -0.15625 to 0.15625
- slot_rows: int32 [16, 192], P('row', 'col'), may hold values from 0 to 12, as said below
- act_cotangent: bfloat16 [4608, 24576], P(('dp', 'row'), 'col'), may hold values from -6 to 6
Outputs:
- activation: bfloat16 [4608, 24576], P(('dp', 'row'), 'col')
- token_grad: bfloat16 [4608, 6144], P(('dp', 'col'), 'row')
- slot_grad: float32 [512, 4, 24576], P('dp', 'row', 'col')
Inputs may be any that keep to these rules, and one draw needn't show every extreme that they name: `slot_rows`: each entry names a block row 0 to 11 of its grid row's feature range, or 12 for an empty slot; the filled slots of one block column name different block rows; the number of filled slots differs between block columns and between grid tiles, and in every tile of 4 x 24576 / 768 entries some block column has all 4 slots filled.
All inputs are finite; a program needn't handle non-finite values.
Results may differ from a plain program's by a relative error of at most 0.023.
Values may be sent and summed in bfloat16 or wider, within the bound.
A program may use at most 64 MiB of HBM per device.

v0:
```python
import jax
import jax.numpy as jnp
from jax import lax
from jax.sharding import PartitionSpec as P

root_two_pi = 0.7978845608028654
cubic_coef = 0.044715


def gelu_pair(hidden):
    inner = root_two_pi * (hidden + cubic_coef * hidden * hidden * hidden)
    tangent = jnp.tanh(inner)
    value = 0.5 * hidden * (1.0 + tangent)
    slope = 0.5 * (1.0 + tangent) + 0.5 * hidden * (1.0 - tangent * tangent) * root_two_pi * (
        1.0 + 3.0 * cubic_coef * hidden * hidden
    )
    return (value, slope)


def body(tokens_in, slot_values, slot_rows, act_cotangent):
    gathered = lax.all_gather(tokens_in, "col", axis=0, tiled=True)
    group_rows, tile_width = gathered.shape
    slot_count, col_blocks = slot_rows.shape
    block_size = slot_values.shape[0] // slot_count
    row_blocks = tile_width // block_size
    selector = (
        slot_rows[:, :, None] == jnp.arange(row_blocks, dtype=jnp.int32)[None, None, :]
    ).astype(jnp.bfloat16)
    slot_vals = slot_values.reshape(slot_count, block_size, col_blocks, block_size)
    picked = jnp.einsum(
        "tbk,sjb->tjsk",
        gathered.reshape(group_rows, row_blocks, block_size),
        selector,
        preferred_element_type=jnp.float32,
    ).astype(jnp.bfloat16)
    own_rows = act_cotangent.shape[0]
    chosen = picked
    partial_sum = jnp.einsum(
        "tjsk,skjn->tjn", chosen, slot_vals, preferred_element_type=jnp.float32
    )
    hidden = lax.psum_scatter(
        partial_sum.reshape(own_rows * lax.axis_size("row"), col_blocks * block_size).astype(
            jnp.bfloat16
        ),
        "row",
        scatter_dimension=0,
        tiled=True,
    ).astype(jnp.float32)
    value, slope = gelu_pair(hidden)
    activation = value.astype(jnp.bfloat16)
    own_grad = (act_cotangent.astype(jnp.float32) * slope).astype(jnp.bfloat16)
    hidden_grad = lax.all_gather(own_grad, "row", axis=0, tiled=True)
    dense_tile = jnp.einsum(
        "sjb,skjn->bkjn", selector, slot_vals, preferred_element_type=jnp.float32
    ).astype(jnp.bfloat16)
    dense_tile = dense_tile.reshape(row_blocks * block_size, col_blocks * block_size)
    chosen = hidden_grad
    token_grad = lax.psum_scatter(
        lax.dot_general(
            chosen, dense_tile, (((1,), (1,)), ((), ())), preferred_element_type=jnp.float32
        ).astype(jnp.bfloat16),
        "col",
        scatter_dimension=0,
        tiled=True,
    )
    grad_blocks = hidden_grad.reshape(group_rows, col_blocks, block_size)
    picked_flat = picked.reshape(group_rows, col_blocks, slot_count * block_size)
    share_rows = slot_values.shape[0] // lax.axis_size("dp")
    chosen = picked_flat
    term = jnp.einsum("tjm,tjn->mjn", chosen, grad_blocks, preferred_element_type=jnp.float32)
    summed = lax.psum_scatter(
        term.reshape(share_rows * lax.axis_size("dp"), col_blocks * block_size).astype(
            jnp.bfloat16
        ),
        "dp",
        scatter_dimension=0,
        tiled=True,
    ).astype(jnp.float32)
    factor = float(group_rows * lax.axis_size("dp")) ** (-0.5)
    slot_grad = (summed * factor).reshape(share_rows, 1, col_blocks * block_size)
    return (activation, token_grad, slot_grad)


def solution(mesh):
    return jax.shard_map(
        body,
        mesh=mesh,
        in_specs=(
            P(("dp", "col"), "row"),
            P("row", "col"),
            P("row", "col"),
            P(("dp", "row"), "col"),
        ),
        out_specs=(P(("dp", "row"), "col"), P(("dp", "col"), "row"), P("dp", "row", "col")),
        check_vma=False,
    )
```

profile of v0, /device:TPU:1, one launch (start us, length us, event | category | flops | bytes accessed | tf_op | source)
XLA Modules:
  0.0 424.6 jit_solution(13758683505072643554)
XLA Ops:
  7.2 0.0 all-gather.3.cloned.1.call-start
  7.2 0.8 copy.24
  8.0 0.1 fusion.34
  8.1 27.0 %all_gather.6 = bf16[144,1536]{1,0:T(8,128)(2,1)S(1)} all-gather(bf16[24,1536]{1,0:T(8,128)(2,1)} %param.4), channel_id=1, replica_groups=mesh['dp'=32,'row'=4,'col'=6] {'col'}, dimensions={0}, use_global_device_ids=true | all-gather | bytes 516096 | tf_op jit(solution)/shard_map/all_gather | solution.py:21
  35.0 0.3 reshape.39
  35.4 3.4 copy.43
  38.8 1.4 convert_bitcast_fusion.1
  40.2 7.5 %fusion.15 = bf16[32,18,8,128]{3,2,1,0:T(8,128)(2,1)S(1)} fusion(bf16[4,128,32,128]{3,2,1,0:T(8,128)(2,1)S(1)} %bitcast.45, bf16[144,32,4,128]{3,1,0,2:T(8,128)(2,1)S(1)} %convert_bitcast_fusion.1), kind=kOutput, calls=%fused_computation.19 | convolution fusion | flops 604569600 | bytes 10092544 | tf_op jit(solution)/shard_map/tjsk,skjn->tjn/dot_general | solution.py:38
  47.7 0.3 copy.70
  48.0 28.6 %fusion = bf16[40,4096]{1,0:T(8,128)(2,1)S(1)} fusion(bf16[144,4096]{1,0:T(8,128)(2,1)S(1)} %bitcast.49), kind=kCustom, calls=%all-reduce-scatter | all-reduce-scatter fusion | flops 655361 | bytes 1511424
  76.7 1.6 collective-permute-start
  78.3 1.3 dynamic-slice.4
  80.2 0.4 concatenate
  80.7 1.4 fusion.32
  82.0 0.0 all-gather.3.cloned.1.call-update
  82.1 0.0 reduce-scatter.7.cloned.1.call-start
  82.1 8.1 %copy.40 = bf16[144,32,4,128]{3,2,0,1:T(4,128)(2,1)} copy(bf16[144,32,4,128]{3,1,0,2:T(8,128)(2,1)} %copy-done.1) | data formatting | bytes 9437184 | tf_op jit(solution)/shard_map/reshape | solution.py:67
  90.3 8.1 %reshape.43 = bf16[144,32,512]{2,0,1:T(8,128)(2,1)} reshape(bf16[144,32,4,128]{3,2,0,1:T(4,128)(2,1)} %copy.40) | data formatting | bytes 9437184 | tf_op jit(solution)/shard_map/reshape | solution.py:67
  98.3 27.3 %all-gather.3.cloned.1.call-done = bf16[4,36,4096]{2,1,0:T(8,128)(2,1)} async-done(((bf16[1,36,4096]{2,1,0:T(8,128)(2,1)}), bf16[4,36,4096]{2,1,0:T(8,128)(2,1)}) %all-gather.3.cloned.1.call-update) | async-done | bytes 1179664 | tf_op jit(solution)/shard_map/all_gather | solution.py:52
  125.6 1.8 reshape.32
  127.4 5.8 %convolution_convert_fusion = bf16[32,128,512]{2,1,0:T(8,128)(2,1)} fusion(bf16[144,32,512]{2,0,1:T(8,128)(2,1)} %reshape.43, bf16[144,32,128]{2,1,0:T(8,128)(2,1)S(1)} %reshape.32), kind=kOutput, calls=%fused_computation.9 | convolution fusion | flops 606076928 | bytes 10092544 | tf_op jit(solution)/shard_map/tjm,tjn->mjn/dot_general | solution.py:70
  133.2 6.4 %copy.34 = bf16[512,4096]{1,0:T(8,128)(2,1)} copy(bf16[512,4096]{0,1:T(8,128)(2,1)} %bitcast.47) | data formatting | bytes 8388608 | tf_op jit(solution)/shard_map/convert_element_type | solution.py:72
  139.6 0.0 reduce-scatter.7.cloned.1.call-update
  139.6 0.0 reduce-scatter.5.cloned.1.call-start
  139.7 11.4 %convert_bitcast_fusion = bf16[12,128,32,128]{3,0,1,2:T(8,128)(2,1)S(1)} fusion(bf16[4,128,32,128]{3,2,1,0:T(8,128)(2,1)} %bitcast.46, s32[4,32]{0,1:T(8,128)S(1)} %copy.24), kind=kOutput, calls=%fused_computation | convolution fusion | flops 56624640 | bytes 16777728 | tf_op jit(solution)/shard_map/sjb,skjn->bkjn/dot_general | solution.py:53
  151.1 16.8 %copy.30 = bf16[12,128,32,128]{3,2,1,0:T(8,128)(2,1)} copy(bf16[12,128,32,128]{3,0,1,2:T(8,128)(2,1)S(1)} %convert_bitcast_fusion) | data formatting | bytes 25165824 | tf_op jit(solution)/shard_map/convert_element_type | solution.py:55
  168.0 0.5 reshape.36
  168.5 12.3 %fusion.8 = bf16[144,1536]{1,0:T(8,128)(2,1)} fusion(bf16[144,4096]{1,0:T(8,128)(2,1)S(1)} %reshape.36, bf16[192,8,32,128]{3,2,1,0:T(8,128)(2,1)} %bitcast.48), kind=kOutput, calls=%fused_computation.10 | convolution fusion | flops 1812160512 | bytes 14204928 | tf_op jit(solution)/shard_map/dot_general | solution.py:59
  180.8 186.1 %reduce-scatter.7.cloned.1.call-done = bf16[16,4096]{1,0:T(8,128)(2,1)} async-done(((bf16[512,4096]{1,0:T(8,128)(2,1)}), bf16[16,4096]{1,0:T(8,128)(2,1)}) %reduce-scatter.7.cloned.1.call-update) | async-done | bytes 131088 | tf_op jit(solution)/shard_map/reduce_scatter | solution.py:71
  366.9 0.9 convert_multiply_fusion.6
  367.9 1.0 reshape.34
  368.8 49.2 %reduce-scatter.5.cloned.1.call-done = bf16[24,1536]{1,0:T(8,128)(2,1)} async-done(((bf16[144,1536]{1,0:T(8,128)(2,1)}), bf16[24,1536]{1,0:T(8,128)(2,1)}) %reduce-scatter.5.cloned.1.call-update) | async-done | bytes 73744 | tf_op jit(solution)/shard_map/reduce_scatter | solution.py:58
  (11 shorter events, 0.1 us)
Async XLA Ops:
  7.2 118.4 %all-gather.3.cloned.1.call-start = ((), (), s32[]{:S(2)}) async-start(), calls=%async_computation.4 | async-start | bytes 1638400 | tf_op jit(solution)/shard_map/all_gather | solution.py:52
  38.8 8.9 %copy-start = (bf16[64,8,32,128]{3,2,1,0:T(8,128)(2,1)}, bf16[64,8,32,128]{3,2,1,0:T(8,128)(2,1)S(1)}, u32[]{:S(2)}) copy-start(bf16[64,8,32,128]{3,2,1,0:T(8,128)(2,1)S(1)} %copy.43) | copy-start | bytes 12582916
  40.2 7.5 %copy-start.1 = (bf16[144,32,4,128]{3,1,0,2:T(8,128)(2,1)}, bf16[144,32,4,128]{3,1,0,2:T(8,128)(2,1)S(1)}, u32[]{:S(2)}) copy-start(bf16[144,32,4,128]{3,1,0,2:T(8,128)(2,1)S(1)} %convert_bitcast_fusion.1) | copy-start | bytes 14155780
  47.7 33.0 %copy-start.3 = (bf16[36,4096]{1,0:T(8,128)(2,1)S(1)}, bf16[36,4096]{1,0:T(8,128)(2,1)}, u32[]{:S(2)}) copy-start(bf16[36,4096]{1,0:T(8,128)(2,1)} %param.7) | copy-start | bytes 884740
  76.7 3.5 collective-permute-start
  82.1 284.9 %reduce-scatter.7.cloned.1.call-start = ((), (), s32[]{:S(2)}) async-start(), calls=%async_computation.3 | async-start | bytes 4325376 | tf_op jit(solution)/shard_map/reduce_scatter | solution.py:71
  139.6 278.4 %reduce-scatter.5.cloned.1.call-start = ((), (), s32[]{:S(2)}) async-start(), calls=%async_computation.2 | async-start | bytes 516096 | tf_op jit(solution)/shard_map/reduce_scatter | solution.py:58
  151.1 16.8 %copy-start.2 = (bf16[4,36,4096]{2,1,0:T(8,128)(2,1)S(1)}, bf16[4,36,4096]{2,1,0:T(8,128)(2,1)}, u32[]{:S(2)}) copy-start(bf16[4,36,4096]{2,1,0:T(8,128)(2,1)} %all-gather.3.cloned.1.call-done) | copy-start | bytes 3538948
Sparse Core Ops, SparseCore 0:
  82.2 43.3 all-gather.2
  139.7 227.1 reduce-scatter.6
  370.9 47.0 reduce-scatter.4
where the time goes:
time: 425 us
  waiting for transfers between devices  263 us (62%)
  blocking collectives  55.6 us (13%)
  local copies, waits for them, and re-layouts  49.2 us (12%)
  matrix products  38.4 us (9%)
  between operations  14.6 us (3%)
    reduce_scatter x1, waiting for transfers between devices, body(): lax.psum_scatter(term.reshape(share_rows * lax.axis_size('dp'), col_block...  186 us
    reduce_scatter x1, waiting for transfers between devices, body(): lax.psum_scatter(lax.dot_general(chosen, dense_tile, (((1,), (1,)), ((),...  49.2 us
    unnamed x1, blocking collectives  28.6 us
    all_gather x1, waiting for transfers between devices, body(): hidden_grad = lax.all_gather(own_grad, 'row', axis=0, tiled=True)  27.3 us
    all_gather x1, blocking collectives, body(): gathered = lax.all_gather(tokens_in, 'col', axis=0, tiled=True)  27 us
    convert_element_type x1, local copies, waits for them, and re-layouts, body(): dense_tile = jnp.einsum('sjb,skjn->bkjn', selector, slot_vals, preferred_...  16.8 us
    reshape x2, local copies, waits for them, and re-layouts, body(): picked.reshape(group_rows, col_blocks, slot_count * block_size)  16.2 us
    dot_general x1, matrix products, body(): lax.dot_general(chosen, dense_tile, (((1,), (1,)), ((), ())), preferred_e...  12.3 us
  transfers between devices with their start and end apart: 4, of which 3 were waited for; matrix products, arithmetic and copies ran while one was open for 14% of the time, Pallas kernels for 0%

commit v1 on v0

v1 whole, which is shorter than its diff:
```python
import jax
import jax.numpy as jnp
from jax import lax
from jax.experimental import pallas as pl
from jax.experimental.pallas import tpu as pltpu
from jax.sharding import PartitionSpec as P

MESH = pl.DeviceIdType.MESH
BF16 = jnp.bfloat16
F32 = jnp.float32

BLK = 128
CAP = 4
BT = 12
COLS = 32
X, Y = 4, 8
R = 4
Z = 3
TOK = 144
NC = 8
NJ = COLS // NC
NB = NJ // 2

root_two_pi = 0.7978845608028654
cubic_coef = 0.044715


def gelu_pair(hidden):
    inner = root_two_pi * (hidden + cubic_coef * hidden * hidden * hidden)
    tangent = jnp.tanh(inner)
    value = 0.5 * hidden * (1.0 + tangent)
    slope = 0.5 * (1.0 + tangent) + 0.5 * hidden * (1.0 - tangent * tangent) * root_two_pi * (
        1.0 + 3.0 * cubic_coef * hidden * hidden
    )
    return (value, slope)


class Ring:
    def __init__(self, total, first, later, size, here, right, left, send, recv, base):
        self.total, self.first, self.later = total, first, later
        self.size, self.here, self.right, self.left = size, here, right, left
        self.send, self.recv, self.base = send, recv, base
        self.half = size // 2

    def shard(self, k, step, way):
        offset = self.half + 1 - step
        place = lax.rem(self.here + (offset if way == 0 else self.size - offset), self.size)
        ref = self.total.at[k, place]
        if step == 1:
            part = self.total.shape[2] // 2
            return ref.at[pl.ds(way * part, part)]
        return ref

    def landing(self, k, step, way):
        return self.first.at[k, way] if step == 1 else self.later.at[k, step - 2, way]

    def copy(self, k, step, way):
        kind = self.base + 2 * (step - 1) + way
        return pltpu.make_async_remote_copy(
            src_ref=self.shard(k, step, way),
            dst_ref=self.landing(k, step, way),
            send_sem=self.send.at[kind],
            recv_sem=self.recv.at[k, kind],
            device_id=self.right if way == 0 else self.left,
            device_id_type=MESH,
        )

    def drain(self, k, step):
        for way in range(2):
            self.copy(k, step, way).wait_send()

    def advance(self, k, step):
        for way in range(2):
            if step > 1:
                self.copy(k, step - 1, way).wait_recv()
                ref = self.shard(k, step, way)
                if step == 2:
                    part = self.total.shape[2] // 2
                    ref = ref.at[pl.ds(way * part, part)]
                got = self.landing(k, step - 1, way)
                ref[...] = (ref[...].astype(F32) + got[...].astype(F32)).astype(BF16)
            self.copy(k, step, way).start()
        if step > 1:
            self.drain(k, step - 1)

    def finish(self, k):
        last = self.half
        for way in range(2):
            self.copy(k, last, way).wait_recv()
        result = self.total[k, self.here].astype(F32)
        result = result + self.landing(k, last, 0)[...].astype(F32)
        result = result + self.landing(k, last, 1)[...].astype(F32)
        self.drain(k, last)
        return result


def kernel(
    tok_in, rows, inv, cot_in, sv_hbm,
    act_out, tg_out, sg_out,
    agb, tok, tokt, sv, cot, part, rr, rl, hg,
    ta, ax1, ax2, ya, ay1, ay2, tb, by1, by2, xb, bx1, bx2,
    tgacc, tgs, tgr1, tgr2,
    sv_sem, tk_send, tk_recv, row_send, row_recv, ring_send, ring_recv, tg_send, tg_recv,
):
    dp, row, col = lax.axis_index("dp"), lax.axis_index("row"), lax.axis_index("col")
    x, y = lax.rem(dp, X), lax.div(dp, X)
    core, z = lax.rem(col, 2), lax.div(col, 2)
    x_right = (y * X + lax.rem(x + 1, X), row, col)
    x_left = (y * X + lax.rem(x + X - 1, X), row, col)
    y_right = (lax.rem(y + 1, Y) * X + x, row, col)
    y_left = (lax.rem(y + Y - 1, Y) * X + x, row, col)
    row_right, row_left = (dp, row + 1, col), (dp, row - 1, col)
    sibling = (dp, row, z * 2 + 1 - core)
    z_right, z_left = lax.rem(z + 1, Z), lax.rem(z + Z - 1, Z)
    dev_z_right, dev_z_left = (dp, row, z_right * 2 + core), (dp, row, z_left * 2 + core)

    load = pltpu.make_async_copy(sv_hbm, sv.at[pl.ds(0, CAP)], sv_sem)
    load.start()

    barrier = pltpu.get_barrier_semaphore()
    for other in (x_right, x_left, y_right, y_left, sibling, dev_z_right, dev_z_left):
        pl.semaphore_signal(barrier, inc=1, device_id=other, device_id_type=MESH)

    @pl.when(row < R - 1)
    def _():
        pl.semaphore_signal(barrier, inc=1, device_id=row_right, device_id_type=MESH)

    @pl.when(row > 0)
    def _():
        pl.semaphore_signal(barrier, inc=1, device_id=row_left, device_id_type=MESH)

    own = tok_in[...].astype(F32)
    for p in range(BT // 2):
        pair = [own[:, (2 * p + i) * BLK : (2 * p + i + 1) * BLK] for i in range(2)]
        agb[col, pl.ds(3 * p, 3)] = jnp.concatenate(pair, 0).astype(BF16).reshape(3, 16, BLK)

    pl.semaphore_wait(barrier, 7 + (row < R - 1).astype(jnp.int32) + (row > 0).astype(jnp.int32))

    def token_copy(slot, send, device):
        return pltpu.make_async_remote_copy(
            src_ref=agb.at[slot],
            dst_ref=agb.at[slot],
            send_sem=tk_send.at[send],
            recv_sem=tk_recv.at[slot],
            device_id=device,
            device_id_type=MESH,
        )

    token_copy(col, 0, dev_z_right).start()
    token_copy(col, 1, dev_z_left).start()
    token_copy(col, 2, sibling).start()

    last_rows = cot_in[pl.ds(32, 4), :].astype(F32)
    for k in range(NC):
        for jj in range(NJ):
            j = k * NJ + jj
            cot[k, pl.ds(2 * jj, 2)] = cot_in[pl.ds(0, 32), pl.ds(j * BLK, BLK)].reshape(2, 16, BLK)
        cot[k, 2 * NJ] = jnp.concatenate(
            [last_rows[:, (k * NJ + jj) * BLK : (k * NJ + jj + 1) * BLK] for jj in range(NJ)], 0
        ).astype(BF16)
    sv[CAP] = jnp.zeros((BLK, COLS * BLK), BF16)
    rr[:, 0] = jnp.zeros((NC, 2 * NJ + 1, 16, BLK), BF16)
    rl[:, R - 1] = jnp.zeros((NC, 2 * NJ + 1, 16, BLK), BF16)
    tgacc[...] = jnp.zeros(tgacc.shape, F32)
    tok[BT] = jnp.zeros((TOK, BLK), BF16)
    tokt[BT] = jnp.zeros((BLK, 2 * BLK), BF16)

    from_left, from_right = z_left * 2 + core, z_right * 2 + core
    token_copy(from_left, 0, dev_z_right).wait_recv()
    token_copy(from_left, 3, sibling).start()
    token_copy(from_right, 0, dev_z_left).wait_recv()
    token_copy(from_right, 4, sibling).start()
    for other in range(Z):
        token_copy(other * 2 + 1 - core, 2, sibling).wait_recv()
    for send in range(5):
        token_copy(col, send, sibling).wait_send()

    def unpack(p, carry):
        pieces = [agb[c, pl.ds(3 * p, 3)].astype(F32).reshape(48, BLK) for c in range(2 * Z)]
        for i in range(2):
            full = jnp.concatenate([v[24 * i : 24 * i + 24] for v in pieces], 0)
            ordered = jnp.concatenate(
                [full[36 * r : 36 * r + 32] for r in range(R)]
                + [full[36 * r + 32 : 36 * r + 36] for r in range(R)]
                + [jnp.zeros((2 * BLK - TOK, BLK), F32)],
                0,
            )
            tok[2 * p + i] = ordered[:TOK].astype(BF16)
            tokt[2 * p + i] = ordered.T.astype(BF16)
        return carry

    lax.fori_loop(0, BT // 2, unpack, 0)
    load.wait()

    ring_ax = Ring(ta, ax1, ax2, X, x, x_right, x_left, ring_send, ring_recv, 0)
    ring_ay = Ring(ya, ay1, ay2, Y, y, y_right, y_left, ring_send, ring_recv, 4)
    ring_by = Ring(tb, by1, by2, Y, y, y_right, y_left, ring_send, ring_recv, 12)
    ring_bx = Ring(xb, bx1, bx2, X, x, x_right, x_left, ring_send, ring_recv, 20)

    def columns(j):
        return pl.ds(pl.multiple_of(j * BLK, BLK), BLK)

    def row_sum_copy(k, step, way):
        if way == 0:
            dests, land, device = pl.ds(step, R - step), rr, row_right
        else:
            dests, land, device = pl.ds(0, R - step), rl, row_left
        return pltpu.make_async_remote_copy(
            src_ref=part.at[k, dests],
            dst_ref=land.at[k, dests],
            send_sem=row_send.at[way],
            recv_sem=row_recv.at[k, way],
            device_id=device,
            device_id_type=MESH,
        )

    def row_sum_drain(k, step):
        @pl.when(row == step - 1)
        def _():
            row_sum_copy(k, step, 0).wait_send()

        @pl.when(row == R - step)
        def _():
            row_sum_copy(k, step, 1).wait_send()

    def row_sum(k, step):
        @pl.when(row == step - 1)
        def _():
            if step > 1:
                row_sum_copy(k, step - 1, 0).wait_recv()
                dests = pl.ds(step, R - step)
                part[k, dests] = (part[k, dests].astype(F32) + rr[k, dests].astype(F32)).astype(BF16)
            row_sum_copy(k, step, 0).start()

        @pl.when(row == R - step)
        def _():
            if step > 1:
                row_sum_copy(k, step - 1, 1).wait_recv()
                dests = pl.ds(0, R - step)
                part[k, dests] = (part[k, dests].astype(F32) + rl[k, dests].astype(F32)).astype(BF16)
            row_sum_copy(k, step, 1).start()

        if step > 1:
            row_sum_drain(k, step - 1)

    def gather_copy(k, source, step, way):
        return pltpu.make_async_remote_copy(
            src_ref=hg.at[k, source],
            dst_ref=hg.at[k, source],
            send_sem=row_send.at[2 + 2 * step + way],
            recv_sem=row_recv.at[k, 2 + source],
            device_id=row_right if way == 0 else row_left,
            device_id_type=MESH,
        )

    def gather_sources(step):
        return (
            (0, row - step, (row >= step), row < R - 1),
            (1, row + step, (row + step < R), row > 0),
        )

    def gather_drain(k, step):
        for way, source, have, onward in gather_sources(step):

            @pl.when(have & onward)
            def _():
                gather_copy(k, source, step, way).wait_send()

    def gather(k, step):
        for way, source, have, onward in gather_sources(step):
            if step > 0:

                @pl.when(have)
                def _():
                    gather_copy(k, source, step - 1, way).wait_recv()

            if step < R - 1:

                @pl.when(have & onward)
                def _():
                    gather_copy(k, source, step, way).start()

        if step > 0:
            gather_drain(k, step - 1)

    def forward(k):
        ends = []
        for jj in range(NJ):
            j = k * NJ + jj
            picked = jnp.concatenate([tok[rows[s, j]] for s in range(CAP)], 1)
            weight = sv[pl.ds(0, CAP), :, columns(j)].reshape(CAP * BLK, BLK)
            result = jnp.dot(picked, weight, preferred_element_type=F32)
            for d in range(R):
                part[k, d, pl.ds(2 * jj, 2)] = result[32 * d : 32 * d + 32].astype(BF16).reshape(2, 16, BLK)
            ends.append(result[32 * R :])
        for d in range(R):
            part[k, d, 2 * NJ] = jnp.concatenate([e[4 * d : 4 * d + 4] for e in ends], 0).astype(BF16)
        row_sum(k, 1)

    def activate(k):
        @pl.when(row == R - 1)
        def _():
            row_sum_copy(k, R - 1, 0).wait_recv()

        @pl.when(row == 0)
        def _():
            row_sum_copy(k, R - 1, 1).wait_recv()

        hidden = part[k, row].astype(F32) + rr[k, row].astype(F32) + rl[k, row].astype(F32)
        value, slope = gelu_pair(hidden)
        hg[k, row] = (cot[k].astype(F32) * slope).astype(BF16)
        gather(k, 0)
        act_out[k] = value.astype(BF16)
        row_sum_drain(k, R - 1)

    def grad_blocks(k):
        ends = [hg[k, s, 2 * NJ].astype(F32) for s in range(R)]
        blocks = []
        for jj in range(NJ):
            mains = [hg[k, s, pl.ds(2 * jj, 2)].reshape(32, BLK) for s in range(R)]
            end = jnp.concatenate([e[4 * jj : 4 * jj + 4] for e in ends], 0).astype(BF16)
            blocks.append(jnp.concatenate(mains + [end], 0))
        return blocks

    def weight_grad(k):
        blocks = grad_blocks(k)
        for jj in range(NJ):
            j = k * NJ + jj
            picked = jnp.concatenate([tokt[rows[s, j]] for s in range(CAP)], 0)
            grad = jnp.concatenate([blocks[jj], jnp.zeros((2 * BLK - TOK, BLK), BF16)], 0)
            term = jnp.dot(picked, grad, preferred_element_type=F32).astype(BF16).reshape(Y, X, 16, BLK)
            if jj < NB:
                for xx in range(X):
                    ta[k, xx, :, jj] = term[:, xx]
            else:
                tb[k, :, :, jj - NB] = term
        ring_ax.advance(k, 1)
        ring_by.advance(k, 1)

    def token_grad(k):
        grad = jnp.concatenate(grad_blocks(k), 1)

        def pair(p, carry):
            weights = [
                jnp.concatenate(
                    [sv[inv[2 * p + i, k * NJ + jj], :, columns(k * NJ + jj)] for jj in range(NJ)],
                    1,
                )
                for i in range(2)
            ]
            tgacc[p] += lax.dot_general(
                grad, jnp.concatenate(weights, 0), (((1,), (1,)), ((), ())), preferred_element_type=F32
            )
            return carry

        lax.fori_loop(0, BT // 2, pair, 0)

    def tg_copy(step):
        if step == 0:
            src, dst, device = tgs.at[1 - core], tgr1, sibling
        elif step == 1:
            src, dst, device = tgs.at[core, z_right], tgr2.at[0], dev_z_right
        else:
            src, dst, device = tgs.at[core, z_left], tgr2.at[1], dev_z_left
        return pltpu.make_async_remote_copy(
            src_ref=src,
            dst_ref=dst,
            send_sem=tg_send.at[step],
            recv_sem=tg_recv.at[step],
            device_id=device,
            device_id_type=MESH,
        )

    def tg_first():
        def pair(p, carry):
            both = tgacc[p]
            pieces = []
            for i in range(2):
                v = both[:, i * BLK : (i + 1) * BLK]
                order = []
                for r in range(R):
                    order += [v[32 * r : 32 * r + 32], v[32 * R + 4 * r : 32 * R + 4 * r + 4]]
                pieces.append(jnp.concatenate(order, 0))
            for c in range(2 * Z):
                shard = jnp.concatenate([v[24 * c : 24 * c + 24] for v in pieces], 0)
                tgs[c % 2, c // 2, pl.ds(3 * p, 3)] = shard.astype(BF16).reshape(3, 16, BLK)
            return carry

        lax.fori_loop(0, BT // 2, pair, 0)
        tg_copy(0).start()

    def tg_second():
        tg_copy(0).wait_recv()
        tgs[core] = (tgs[core].astype(F32) + tgr1[...].astype(F32)).astype(BF16)
        tg_copy(1).start()
        tg_copy(2).start()
        tg_copy(0).wait_send()

    def tg_last():
        tg_copy(1).wait_recv()
        tg_copy(2).wait_recv()
        total = tgs[core, z].astype(F32) + tgr2[0].astype(F32) + tgr2[1].astype(F32)
        tg_out[...] = total.astype(BF16)
        tg_copy(1).wait_send()
        tg_copy(2).wait_send()

    factor = float(TOK * X * Y) ** (-0.5)

    def ring_7(k):
        ring_ax.advance(k, 2)
        ring_by.advance(k, 2)

    def ring_8(k):
        ya[k] = ring_ax.finish(k).astype(BF16)
        ring_ay.advance(k, 1)
        ring_by.advance(k, 3)

    def ring_9(k):
        ring_ay.advance(k, 2)
        ring_by.advance(k, 4)

    def ring_10(k):
        xb[k] = ring_by.finish(k).astype(BF16)
        ring_bx.advance(k, 1)
        ring_ay.advance(k, 3)

    def ring_11(k):
        ring_ay.advance(k, 4)
        ring_bx.advance(k, 2)

    def ring_12(k):
        left = ring_ay.finish(k) * factor
        right = ring_bx.finish(k) * factor
        for b in range(NB):
            sg_out[:, columns(k * NJ + b)] = left[b]
            sg_out[:, columns(k * NJ + NB + b)] = right[b]

    stages = (
        (6, lambda k: gather(k, 3)),
        (5, lambda k: gather(k, 2)),
        (4, lambda k: gather(k, 1)),
        (3, activate),
        (2, lambda k: row_sum(k, 3)),
        (1, lambda k: row_sum(k, 2)),
        (12, ring_12),
        (11, ring_11),
        (10, ring_10),
        (9, ring_9),
        (8, ring_8),
        (7, ring_7),
        (6, weight_grad),
        (0, forward),
        (6, token_grad),
    )

    def tick(t, carry):
        for stage, work in stages:
            k = t - stage

            @pl.when((k >= 0) & (k < NC))
            def _():
                work(k)

        for at, work in ((6, tg_first), (7, tg_second), (8, tg_last)):

            @pl.when(t == NC + at)
            def _():
                work()

        return carry

    lax.fori_loop(0, NC + 12, tick, 0)


def body(tokens_in, slot_values, slot_rows, act_cotangent):
    blocks = jnp.arange(BT, dtype=jnp.int32)
    slots = jnp.arange(CAP, dtype=jnp.int32)
    match = slot_rows[None, :, :] == blocks[:, None, None]
    inverse = CAP + jnp.sum(jnp.where(match, slots[None, :, None] - CAP, 0), axis=1)

    def dma(*shape):
        return pltpu.SemaphoreType.DMA(shape)

    def buf(*shape, dtype=BF16):
        return pltpu.VMEM(shape, dtype)

    vmem = pl.BlockSpec(memory_space=pltpu.VMEM)
    smem = pl.BlockSpec(memory_space=pltpu.SMEM)
    tiles = 2 * NJ + 1
    packed, grad, summed = pl.pallas_call(
        kernel,
        out_shape=(
            jax.ShapeDtypeStruct((NC, tiles, 16, BLK), BF16),
            jax.ShapeDtypeStruct((18, 16, BLK), BF16),
            jax.ShapeDtypeStruct((16, COLS * BLK), F32),
        ),
        in_specs=[vmem, smem, smem, vmem, pl.BlockSpec(memory_space=pl.ANY)],
        out_specs=(vmem, vmem, vmem),
        scratch_shapes=[
            buf(2 * Z, 18, 16, BLK),
            buf(BT + 1, TOK, BLK),
            buf(BT + 1, BLK, 2 * BLK),
            buf(CAP + 1, BLK, COLS * BLK),
            buf(NC, tiles, 16, BLK),
            buf(NC, R, tiles, 16, BLK),
            buf(NC, R, tiles, 16, BLK),
            buf(NC, R, tiles, 16, BLK),
            buf(NC, R, tiles, 16, BLK),
            buf(NC, X, Y, NB, 16, BLK),
            buf(NC, 2, Y // 2, NB, 16, BLK),
            buf(NC, 1, 2, Y, NB, 16, BLK),
            buf(NC, Y, NB, 16, BLK),
            buf(NC, 2, NB // 2, 16, BLK),
            buf(NC, 3, 2, NB, 16, BLK),
            buf(NC, Y, X, NB, 16, BLK),
            buf(NC, 2, X // 2, NB, 16, BLK),
            buf(NC, 3, 2, X, NB, 16, BLK),
            buf(NC, X, NB, 16, BLK),
            buf(NC, 2, NB // 2, 16, BLK),
            buf(NC, 1, 2, NB, 16, BLK),
            buf(BT // 2, TOK, 2 * BLK, dtype=F32),
            buf(2, Z, 18, 16, BLK),
            buf(Z, 18, 16, BLK),
            buf(2, 18, 16, BLK),
            pltpu.SemaphoreType.DMA,
            dma(5),
            dma(2 * Z),
            dma(8),
            dma(NC, 6),
            dma(24),
            dma(NC, 24),
            dma(3),
            dma(3),
        ],
        compiler_params=pltpu.CompilerParams(
            collective_id=0, has_side_effects=True, vmem_limit_bytes=52 * 1024 * 1024
        ),
    )(tokens_in, slot_rows, inverse, act_cotangent, slot_values.reshape(CAP, BLK, COLS * BLK))

    mains = packed[:, : 2 * NJ].reshape(NC, NJ, 32, BLK)
    ends = packed[:, 2 * NJ].reshape(NC, NJ, 4, BLK)
    activation = jnp.concatenate([mains, ends], axis=2).transpose(2, 0, 1, 3).reshape(36, COLS * BLK)
    token_grad = grad.reshape(BT // 2, 2, 24, BLK).transpose(2, 0, 1, 3).reshape(24, BT * BLK)
    slot_grad = summed.reshape(16, 1, COLS * BLK)
    return (activation, token_grad, slot_grad)


def solution(mesh):
    return jax.shard_map(
        body,
        mesh=mesh,
        in_specs=(
            P(("dp", "col"), "row"),
            P("row", "col"),
            P("row", "col"),
            P(("dp", "row"), "col"),
        ),
        out_specs=(P(("dp", "row"), "col"), P(("dp", "col"), "row"), P("dp", "row", "col")),
        check_vma=False,
    )
```

time: 425 us -> 117 us (0.28)
  the two profiles are of different devices: /device:TPU:1 before, /device:TPU:24 now
where the time goes in v1:
time: 117 us
  Pallas kernels  110 us (94%)
  local copies, waits for them, and re-layouts  5.26 us (4%)
    pallas_call x1, Pallas kernels, body(): pl.pallas_call(kernel, out_shape=(jax.ShapeDtypeStruct((NC, tiles, 16, BL...  110 us
    unnamed x7, local copies, waits for them, and re-layouts  3.5 us

profile of v1, /device:TPU:24, one launch (start us, length us, event | category | flops | bytes accessed | tf_op | source)
XLA Modules:
  0.0 116.6 jit_solution(8064255325605532526)
XLA Ops:
  0.6 0.8 select_reduce_fusion
  1.4 0.0 copy-start
  1.4 1.0 copy-done
  2.4 0.0 copy-start.1
  2.4 0.9 copy-done.1
  3.3 0.0 copy-start.2
  3.3 0.7 copy-done.2
  4.0 109.9 %shard_map.67 = (bf16[8,9,16,128]{3,2,1,0:T(8,128)(2,1)S(1)}, bf16[18,16,128]{2,1,0:T(8,128)(2,1)S(1)}, f32[16,4096]{1,0:T(8,128)S(1)}) custom-call(bf16[24,1536]{1,0:T(8,128)(2,1)S(1)} %copy-done.1, s32[4,32]{1,0:T(4,128)S(1)} %copy-done.2, s32[12,32]{1,0:T(8,128)S(1)} %broadcast_add_fusion.inv, bf16[36,4096]{1,0:T(8,128)(2,1)S(1)} %copy-done, ...), custom_call_target="tpu_custom_call" | custom-call | tf_op jit(solution)/shard_map/pallas_call | solution.py:490
  113.8 0.1 copy.11
  113.9 0.7 reshape.34
  114.6 1.0 copy.12
  115.6 0.1 copy.10
  115.7 0.9 reshape.32
  (5 shorter events, 0.1 us)
Async XLA Ops:
  1.4 1.0 copy-start
  2.4 0.9 copy-start.1
  3.3 0.7 copy-start.2

commit v2 on v1

--- a/solution.py
+++ b/solution.py
@@ -19,7 +19,7 @@
 TOK = 144
 NC = 8
 NJ = COLS // NC
-NB = NJ // 2
+LAG = 2
 
 root_two_pi = 0.7978845608028654
 cubic_coef = 0.044715
@@ -59,7 +59,7 @@
         return pltpu.make_async_remote_copy(
             src_ref=self.shard(k, step, way),
             dst_ref=self.landing(k, step, way),
-            send_sem=self.send.at[kind],
+            send_sem=self.send.at[lax.rem(k, 2), kind],
             recv_sem=self.recv.at[k, kind],
             device_id=self.right if way == 0 else self.left,
             device_id_type=MESH,
@@ -94,12 +94,47 @@
         return result
 
 
+class Direct:
+    def __init__(self, total, landing, size, here, device, send, recv, base):
+        self.total, self.landing, self.size, self.here = total, landing, size, here
+        self.device, self.send, self.recv, self.base = device, send, recv, base
+
+    def copy(self, k, offset):
+        place = lax.rem(self.here + offset, self.size)
+        kind = self.base + offset - 1
+        return pltpu.make_async_remote_copy(
+            src_ref=self.total.at[k, place],
+            dst_ref=self.landing.at[k, offset - 1],
+            send_sem=self.send.at[lax.rem(k, 2), kind],
+            recv_sem=self.recv.at[k, kind],
+            device_id=self.device(place),
+            device_id_type=MESH,
+        )
+
+    def start(self, k):
+        far_first = sorted(range(1, self.size), key=lambda o: -min(o, self.size - o))
+        for offset in far_first:
+            self.copy(k, offset).start()
+
+    def drain(self, k):
+        for offset in range(1, self.size):
+            self.copy(k, offset).wait_send()
+
+    def finish(self, k):
+        for offset in range(1, self.size):
+            self.copy(k, offset).wait_recv()
+        result = self.total[k, self.here].astype(F32)
+        for offset in range(1, self.size):
+            result = result + self.landing[k, offset - 1].astype(F32)
+        return result
+
+
 def kernel(
     tok_in, rows, inv, cot_in, sv_hbm,
     act_out, tg_out, sg_out,
     agb, tok, tokt, sv, cot, part, rr, rl, hg,
-    ta, ax1, ax2, ya, ay1, ay2, tb, by1, by2, xb, bx1, bx2,
-    tgacc, tgs, tgr1, tgr2,
+    ta, ax1, ax2, ya, ay, tb, by1, by2, xb, bx,
+    hgt, tgacc, tgs, tgr1, tgr2,
     sv_sem, tk_send, tk_recv, row_send, row_recv, ring_send, ring_recv, tg_send, tg_recv,
 ):
     dp, row, col = lax.axis_index("dp"), lax.axis_index("row"), lax.axis_index("col")
@@ -118,7 +153,10 @@
     load.start()
 
     barrier = pltpu.get_barrier_semaphore()
-    for other in (x_right, x_left, y_right, y_left, sibling, dev_z_right, dev_z_left):
+    at_x = lambda place: (y * X + place, row, col)
+    at_y = lambda place: (place * X + x, row, col)
+    peers = [at_y(lax.rem(y + o, Y)) for o in range(1, Y)] + [at_x(lax.rem(x + o, X)) for o in range(1, X)]
+    for other in [dev_z_right, dev_z_left] + peers + [sibling]:
         pl.semaphore_signal(barrier, inc=1, device_id=other, device_id_type=MESH)
 
     @pl.when(row < R - 1)
@@ -134,21 +172,23 @@
         pair = [own[:, (2 * p + i) * BLK : (2 * p + i + 1) * BLK] for i in range(2)]
         agb[col, pl.ds(3 * p, 3)] = jnp.concatenate(pair, 0).astype(BF16).reshape(3, 16, BLK)
 
-    pl.semaphore_wait(barrier, 7 + (row < R - 1).astype(jnp.int32) + (row > 0).astype(jnp.int32))
-
-    def token_copy(slot, send, device):
+    pl.semaphore_wait(barrier, X + Y + 1 + (row < R - 1).astype(jnp.int32) + (row > 0).astype(jnp.int32))
+
+    def token_copy(slot, piece, send, device):
+        half = pl.ds(9 * piece, 9)
         return pltpu.make_async_remote_copy(
-            src_ref=agb.at[slot],
-            dst_ref=agb.at[slot],
-            send_sem=tk_send.at[send],
-            recv_sem=tk_recv.at[slot],
+            src_ref=agb.at[slot, half],
+            dst_ref=agb.at[slot, half],
+            send_sem=tk_send.at[piece, send],
+            recv_sem=tk_recv.at[piece, slot],
             device_id=device,
             device_id_type=MESH,
         )
 
-    token_copy(col, 0, dev_z_right).start()
-    token_copy(col, 1, dev_z_left).start()
-    token_copy(col, 2, sibling).start()
+    for piece in range(2):
+        token_copy(col, piece, 0, dev_z_right).start()
+        token_copy(col, piece, 1, dev_z_left).start()
+        token_copy(col, piece, 2, sibling).start()
 
     last_rows = cot_in[pl.ds(32, 4), :].astype(F32)
     for k in range(NC):
@@ -166,15 +206,6 @@
     tokt[BT] = jnp.zeros((BLK, 2 * BLK), BF16)
 
     from_left, from_right = z_left * 2 + core, z_right * 2 + core
-    token_copy(from_left, 0, dev_z_right).wait_recv()
-    token_copy(from_left, 3, sibling).start()
-    token_copy(from_right, 0, dev_z_left).wait_recv()
-    token_copy(from_right, 4, sibling).start()
-    for other in range(Z):
-        token_copy(other * 2 + 1 - core, 2, sibling).wait_recv()
-    for send in range(5):
-        token_copy(col, send, sibling).wait_send()
-
     def unpack(p, carry):
         pieces = [agb[c, pl.ds(3 * p, 3)].astype(F32).reshape(48, BLK) for c in range(2 * Z)]
         for i in range(2):
@@ -189,56 +220,70 @@
             tokt[2 * p + i] = ordered.T.astype(BF16)
         return carry
 
-    lax.fori_loop(0, BT // 2, unpack, 0)
+    for piece in range(2):
+        token_copy(from_left, piece, 0, dev_z_right).wait_recv()
+        token_copy(from_left, piece, 3, sibling).start()
+        token_copy(from_right, piece, 0, dev_z_left).wait_recv()
+        token_copy(from_right, piece, 4, sibling).start()
+        for other in range(Z):
+            token_copy(other * 2 + 1 - core, piece, 2, sibling).wait_recv()
+        lax.fori_loop(3 * piece, 3 * piece + 3, unpack, 0)
+    for piece in range(2):
+        for send in range(5):
+            token_copy(col, piece, send, sibling).wait_send()
     load.wait()
 
     ring_ax = Ring(ta, ax1, ax2, X, x, x_right, x_left, ring_send, ring_recv, 0)
-    ring_ay = Ring(ya, ay1, ay2, Y, y, y_right, y_left, ring_send, ring_recv, 4)
-    ring_by = Ring(tb, by1, by2, Y, y, y_right, y_left, ring_send, ring_recv, 12)
-    ring_bx = Ring(xb, bx1, bx2, X, x, x_right, x_left, ring_send, ring_recv, 20)
+    direct_ay = Direct(ya, ay, Y, y, at_y, ring_send, ring_recv, 4)
+    ring_by = Ring(tb, by1, by2, Y, y, y_right, y_left, ring_send, ring_recv, 11)
+    direct_bx = Direct(xb, bx, X, x, at_x, ring_send, ring_recv, 19)
+
+    def by_path(k, x_first, y_first):
+        y_path = (k == 1) | (k == 4)
+
+        @pl.when(y_path)
+        def _():
+            y_first()
+
+        @pl.when(jnp.logical_not(y_path))
+        def _():
+            x_first()
 
     def columns(j):
         return pl.ds(pl.multiple_of(j * BLK, BLK), BLK)
 
-    def row_sum_copy(k, step, way):
-        if way == 0:
-            dests, land, device = pl.ds(step, R - step), rr, row_right
-        else:
-            dests, land, device = pl.ds(0, R - step), rl, row_left
+    def row_sum_copy(k, dest, way):
         return pltpu.make_async_remote_copy(
-            src_ref=part.at[k, dests],
-            dst_ref=land.at[k, dests],
-            send_sem=row_send.at[way],
-            recv_sem=row_recv.at[k, way],
-            device_id=device,
+            src_ref=part.at[k, dest],
+            dst_ref=(rl if way else rr).at[k, dest],
+            send_sem=row_send.at[lax.rem(k, 2), dest],
+            recv_sem=row_recv.at[k, R * way + dest],
+            device_id=row_left if way else row_right,
             device_id_type=MESH,
         )
 
+    def row_sum_roles(step):
+        return ((0, row == step - 1, range(R - 1, step - 1, -1)), (1, row == R - step, range(R - step)))
+
     def row_sum_drain(k, step):
-        @pl.when(row == step - 1)
-        def _():
-            row_sum_copy(k, step, 0).wait_send()
-
-        @pl.when(row == R - step)
-        def _():
-            row_sum_copy(k, step, 1).wait_send()
+        for way, mine, dests in row_sum_roles(step):
+
+            @pl.when(mine)
+            def _():
+                for dest in dests:
+                    row_sum_copy(k, dest, way).wait_send()
 
     def row_sum(k, step):
-        @pl.when(row == step - 1)
-        def _():
-            if step > 1:
-                row_sum_copy(k, step - 1, 0).wait_recv()
-                dests = pl.ds(step, R - step)
-                part[k, dests] = (part[k, dests].astype(F32) + rr[k, dests].astype(F32)).astype(BF16)
-            row_sum_copy(k, step, 0).start()
-
-        @pl.when(row == R - step)
-        def _():
-            if step > 1:
-                row_sum_copy(k, step - 1, 1).wait_recv()
-                dests = pl.ds(0, R - step)
-                part[k, dests] = (part[k, dests].astype(F32) + rl[k, dests].astype(F32)).astype(BF16)
-            row_sum_copy(k, step, 1).start()
+        for way, mine, dests in row_sum_roles(step):
+
+            @pl.when(mine)
+            def _():
+                for dest in dests:
+                    if step > 1:
+                        row_sum_copy(k, dest, way).wait_recv()
+                        got = (rl if way else rr)[k, dest].astype(F32)
+                        part[k, dest] = (part[k, dest].astype(F32) + got).astype(BF16)
+                    row_sum_copy(k, dest, way).start()
 
         if step > 1:
             row_sum_drain(k, step - 1)
@@ -247,8 +292,8 @@
         return pltpu.make_async_remote_copy(
             src_ref=hg.at[k, source],
             dst_ref=hg.at[k, source],
-            send_sem=row_send.at[2 + 2 * step + way],
-            recv_sem=row_recv.at[k, 2 + source],
+            send_sem=row_send.at[lax.rem(k, 2), R + 2 * step + way],
+            recv_sem=row_recv.at[k, 2 * R + source],
             device_id=row_right if way == 0 else row_left,
             device_id_type=MESH,
         )
@@ -298,13 +343,13 @@
         row_sum(k, 1)
 
     def activate(k):
-        @pl.when(row == R - 1)
+        @pl.when(row > 0)
         def _():
-            row_sum_copy(k, R - 1, 0).wait_recv()
-
-        @pl.when(row == 0)
+            row_sum_copy(k, row, 0).wait_recv()
+
+        @pl.when(row < R - 1)
         def _():
-            row_sum_copy(k, R - 1, 1).wait_recv()
+            row_sum_copy(k, row, 1).wait_recv()
 
         hidden = part[k, row].astype(F32) + rr[k, row].astype(F32) + rl[k, row].astype(F32)
         value, slope = gelu_pair(hidden)
@@ -324,21 +369,32 @@
 
     def weight_grad(k):
         blocks = grad_blocks(k)
+        terms = []
         for jj in range(NJ):
             j = k * NJ + jj
             picked = jnp.concatenate([tokt[rows[s, j]] for s in range(CAP)], 0)
             grad = jnp.concatenate([blocks[jj], jnp.zeros((2 * BLK - TOK, BLK), BF16)], 0)
-            term = jnp.dot(picked, grad, preferred_element_type=F32).astype(BF16).reshape(Y, X, 16, BLK)
-            if jj < NB:
+            term = jnp.dot(picked, grad, preferred_element_type=F32)
+            terms.append(term.astype(BF16).reshape(Y, X, 16, BLK))
+
+        def x_first():
+            for jj in range(NJ):
                 for xx in range(X):
-                    ta[k, xx, :, jj] = term[:, xx]
-            else:
-                tb[k, :, :, jj - NB] = term
-        ring_ax.advance(k, 1)
-        ring_by.advance(k, 1)
+                    ta[k, xx, :, jj] = terms[jj][:, xx]
+            ring_ax.advance(k, 1)
+
+        def y_first():
+            for jj in range(NJ):
+                tb[k, :, :, jj] = terms[jj]
+            ring_by.advance(k, 1)
+
+        by_path(k, x_first, y_first)
+        for jj in range(NJ):
+            grad = jnp.concatenate([blocks[jj].astype(F32), jnp.zeros((2 * BLK - TOK, BLK), F32)], 0)
+            hgt[pl.ds(jj * BLK, BLK), :] = grad.T.astype(BF16)
 
     def token_grad(k):
-        grad = jnp.concatenate(grad_blocks(k), 1)
+        grad = hgt[...]
 
         def pair(p, carry):
             weights = [
@@ -348,12 +404,10 @@
                 )
                 for i in range(2)
             ]
-            tgacc[p] += lax.dot_general(
-                grad, jnp.concatenate(weights, 0), (((1,), (1,)), ((), ())), preferred_element_type=F32
-            )
+            tgacc[p] += jnp.dot(jnp.concatenate(weights, 0), grad, preferred_element_type=F32)
             return carry
 
-        lax.fori_loop(0, BT // 2, pair, 0)
+        lax.fori_loop(0, BT // 2, pair, 0, unroll=True)
 
     def tg_copy(step):
         if step == 0:
@@ -373,7 +427,7 @@
 
     def tg_first():
         def pair(p, carry):
-            both = tgacc[p]
+            both = tgacc[p].T
             pieces = []
             for i in range(2):
                 v = both[:, i * BLK : (i + 1) * BLK]
@@ -406,34 +460,40 @@
 
     factor = float(TOK * X * Y) ** (-0.5)
 
-    def ring_7(k):
-        ring_ax.advance(k, 2)
-        ring_by.advance(k, 2)
-
-    def ring_8(k):
-        ya[k] = ring_ax.finish(k).astype(BF16)
-        ring_ay.advance(k, 1)
-        ring_by.advance(k, 3)
-
-    def ring_9(k):
-        ring_ay.advance(k, 2)
-        ring_by.advance(k, 4)
-
-    def ring_10(k):
-        xb[k] = ring_by.finish(k).astype(BF16)
-        ring_bx.advance(k, 1)
-        ring_ay.advance(k, 3)
-
-    def ring_11(k):
-        ring_ay.advance(k, 4)
-        ring_bx.advance(k, 2)
-
-    def ring_12(k):
-        left = ring_ay.finish(k) * factor
-        right = ring_bx.finish(k) * factor
-        for b in range(NB):
-            sg_out[:, columns(k * NJ + b)] = left[b]
-            sg_out[:, columns(k * NJ + NB + b)] = right[b]
+    def write(k, total):
+        for jj in range(NJ):
+            sg_out[:, columns(k * NJ + jj)] = total[jj] * factor
+
+    def sums_2(k):
+        by_path(k, lambda: ring_ax.advance(k, 2), lambda: ring_by.advance(k, 2))
+
+    def sums_3(k):
+        def x_first():
+            ya[k] = ring_ax.finish(k).astype(BF16)
+            direct_ay.start(k)
+
+        by_path(k, x_first, lambda: ring_by.advance(k, 3))
+
+    def sums_4(k):
+        def x_first():
+            write(k, direct_ay.finish(k))
+            direct_ay.drain(k)
+
+        by_path(k, x_first, lambda: ring_by.advance(k, 4))
+
+    def sums_5(k):
+        def y_first():
+            xb[k] = ring_by.finish(k).astype(BF16)
+            direct_bx.start(k)
+
+        by_path(k, lambda: None, y_first)
+
+    def sums_6(k):
+        def y_first():
+            write(k, direct_bx.finish(k))
+            direct_bx.drain(k)
+
+        by_path(k, lambda: None, y_first)
 
     stages = (
         (6, lambda k: gather(k, 3)),
@@ -442,12 +502,11 @@
         (3, activate),
         (2, lambda k: row_sum(k, 3)),
         (1, lambda k: row_sum(k, 2)),
-        (12, ring_12),
-        (11, ring_11),
-        (10, ring_10),
-        (9, ring_9),
-        (8, ring_8),
-        (7, ring_7),
+        (11, sums_6),
+        (10, sums_5),
+        (9, sums_4),
+        (8, sums_3),
+        (7, sums_2),
         (6, weight_grad),
         (0, forward),
         (6, token_grad),
@@ -455,28 +514,29 @@
 
     def tick(t, carry):
         for stage, work in stages:
-            k = t - stage
+            k = t - stage * LAG
 
             @pl.when((k >= 0) & (k < NC))
             def _():
                 work(k)
 
-        for at, work in ((6, tg_first), (7, tg_second), (8, tg_last)):
-
-            @pl.when(t == NC + at)
+        for stage, work in ((6, tg_first), (7, tg_second)):
+
+            @pl.when(t == NC - 1 + stage * LAG)
             def _():
                 work()
 
         return carry
 
-    lax.fori_loop(0, NC + 12, tick, 0)
+    lax.fori_loop(0, max(NC + 9 * LAG, 5 + 11 * LAG), tick, 0)
+    tg_last()
 
 
 def body(tokens_in, slot_values, slot_rows, act_cotangent):
     blocks = jnp.arange(BT, dtype=jnp.int32)
     slots = jnp.arange(CAP, dtype=jnp.int32)
     match = slot_rows[None, :, :] == blocks[:, None, None]
-    inverse = CAP + jnp.sum(jnp.where(match, slots[None, :, None] - CAP, 0), axis=1)
+    inverse = jnp.min(jnp.where(match, slots[None, :, None], CAP), axis=1)
 
     def dma(*shape):
         return pltpu.SemaphoreType.DMA(shape)
@@ -506,29 +566,28 @@
             buf(NC, R, tiles, 16, BLK),
             buf(NC, R, tiles, 16, BLK),
             buf(NC, R, tiles, 16, BLK),
-            buf(NC, X, Y, NB, 16, BLK),
-            buf(NC, 2, Y // 2, NB, 16, BLK),
-            buf(NC, 1, 2, Y, NB, 16, BLK),
-            buf(NC, Y, NB, 16, BLK),
-            buf(NC, 2, NB // 2, 16, BLK),
-            buf(NC, 3, 2, NB, 16, BLK),
-            buf(NC, Y, X, NB, 16, BLK),
-            buf(NC, 2, X // 2, NB, 16, BLK),
-            buf(NC, 3, 2, X, NB, 16, BLK),
-            buf(NC, X, NB, 16, BLK),
-            buf(NC, 2, NB // 2, 16, BLK),
-            buf(NC, 1, 2, NB, 16, BLK),
-            buf(BT // 2, TOK, 2 * BLK, dtype=F32),
+            buf(NC, X, Y, NJ, 16, BLK),
+            buf(NC, 2, Y // 2, NJ, 16, BLK),
+            buf(NC, 1, 2, Y, NJ, 16, BLK),
+            buf(NC, Y, NJ, 16, BLK),
+            buf(NC, Y - 1, NJ, 16, BLK),
+            buf(NC, Y, X, NJ, 16, BLK),
+            buf(NC, 2, X // 2, NJ, 16, BLK),
+            buf(NC, 3, 2, X, NJ, 16, BLK),
+            buf(NC, X, NJ, 16, BLK),
+            buf(NC, X - 1, NJ, 16, BLK),
+            buf(NJ * BLK, 2 * BLK),
+            buf(BT // 2, 2 * BLK, 2 * BLK, dtype=F32),
             buf(2, Z, 18, 16, BLK),
             buf(Z, 18, 16, BLK),
             buf(2, 18, 16, BLK),
             pltpu.SemaphoreType.DMA,
-            dma(5),
-            dma(2 * Z),
-            dma(8),
-            dma(NC, 6),
-            dma(24),
-            dma(NC, 24),
+            dma(2, 5),
+            dma(2, 2 * Z),
+            dma(2, R + 6),
+            dma(NC, 3 * R),
+            dma(2, 22),
+            dma(NC, 22),
             dma(3),
             dma(3),
         ],

time: 117 us -> 106 us (0.906)
  the two profiles are of different devices: /device:TPU:24 before, /device:TPU:8 now
where the time goes in v2:
time: 106 us
  Pallas kernels  99.4 us (94%)
  local copies, waits for them, and re-layouts  5.26 us (5%)
    pallas_call x1, Pallas kernels, body(): pl.pallas_call(kernel, out_shape=(jax.ShapeDtypeStruct((NC, tiles, 16, BL...  99.4 us
    unnamed x7, local copies, waits for them, and re-layouts  3.5 us

profile of v2, /device:TPU:8, one launch (start us, length us, event | category | flops | bytes accessed | tf_op | source)
XLA Modules:
  0.0 106.0 jit_solution(14927506612441639705)
XLA Ops:
  0.6 0.7 select_reduce_fusion.inv
  1.3 0.0 copy-start
  1.4 1.0 copy-done
  2.3 0.0 copy-start.1
  2.3 0.9 copy-done.1
  3.2 0.0 copy-start.2
  3.2 0.7 copy-done.2
  3.9 99.4 %shard_map.67 = (bf16[8,9,16,128]{3,2,1,0:T(8,128)(2,1)S(1)}, bf16[18,16,128]{2,1,0:T(8,128)(2,1)S(1)}, f32[16,4096]{1,0:T(8,128)S(1)}) custom-call(bf16[24,1536]{1,0:T(8,128)(2,1)S(1)} %copy-done.1, s32[4,32]{1,0:T(4,128)S(1)} %copy-done.2, s32[12,32]{1,0:T(8,128)S(1)} %select_reduce_fusion.inv, bf16[36,4096]{1,0:T(8,128)(2,1)S(1)} %copy-done, ...), custom_call_target="tpu_custom_call" | custom-call | tf_op jit(solution)/shard_map/pallas_call | solution.py:550
  103.3 0.1 copy.11
  103.3 0.7 reshape.29
  104.0 1.0 copy.12
  105.0 0.1 copy.10
  105.1 0.9 reshape.27
  (3 shorter events, 0.1 us)
Async XLA Ops:
  1.3 1.0 copy-start
  2.3 0.9 copy-start.1
  3.2 0.7 copy-start.2

commit v3 on v2

--- a/solution.py
+++ b/solution.py
@@ -1,3 +1,5 @@
+import functools
+
 import jax
 import jax.numpy as jnp
 from jax import lax
@@ -19,7 +21,11 @@
 TOK = 144
 NC = 8
 NJ = COLS // NC
-LAG = 2
+LAG = 1
+X_FIRST = (2, 4, 7)
+Y_FIRST = (2, 4, 6, 8, 11)
+Y_CHUNKS = (0, 3)
+SLOTS = 4
 
 root_two_pi = 0.7978845608028654
 cubic_coef = 0.044715
@@ -59,7 +65,7 @@
         return pltpu.make_async_remote_copy(
             src_ref=self.shard(k, step, way),
             dst_ref=self.landing(k, step, way),
-            send_sem=self.send.at[lax.rem(k, 2), kind],
+            send_sem=self.send.at[lax.rem(k, SLOTS), kind],
             recv_sem=self.recv.at[k, kind],
             device_id=self.right if way == 0 else self.left,
             device_id_type=MESH,
@@ -105,7 +111,7 @@
         return pltpu.make_async_remote_copy(
             src_ref=self.total.at[k, place],
             dst_ref=self.landing.at[k, offset - 1],
-            send_sem=self.send.at[lax.rem(k, 2), kind],
+            send_sem=self.send.at[lax.rem(k, SLOTS), kind],
             recv_sem=self.recv.at[k, kind],
             device_id=self.device(place),
             device_id_type=MESH,
@@ -130,7 +136,7 @@
 
 
 def kernel(
-    tok_in, rows, inv, cot_in, sv_hbm,
+    tok_in, table, cot_in, sv_hbm,
     act_out, tg_out, sg_out,
     agb, tok, tokt, sv, cot, part, rr, rl, hg,
     ta, ax1, ax2, ya, ay, tb, by1, by2, xb, bx,
@@ -239,7 +245,7 @@
     direct_bx = Direct(xb, bx, X, x, at_x, ring_send, ring_recv, 19)
 
     def by_path(k, x_first, y_first):
-        y_path = (k == 1) | (k == 4)
+        y_path = functools.reduce(jnp.logical_or, [k == chunk for chunk in Y_CHUNKS])
 
         @pl.when(y_path)
         def _():
@@ -256,7 +262,7 @@
         return pltpu.make_async_remote_copy(
             src_ref=part.at[k, dest],
             dst_ref=(rl if way else rr).at[k, dest],
-            send_sem=row_send.at[lax.rem(k, 2), dest],
+            send_sem=row_send.at[lax.rem(k, SLOTS), dest],
             recv_sem=row_recv.at[k, R * way + dest],
             device_id=row_left if way else row_right,
             device_id_type=MESH,
@@ -292,7 +298,7 @@
         return pltpu.make_async_remote_copy(
             src_ref=hg.at[k, source],
             dst_ref=hg.at[k, source],
-            send_sem=row_send.at[lax.rem(k, 2), R + 2 * step + way],
+            send_sem=row_send.at[lax.rem(k, SLOTS), R + 2 * step + way],
             recv_sem=row_recv.at[k, 2 * R + source],
             device_id=row_right if way == 0 else row_left,
             device_id_type=MESH,
@@ -332,7 +338,7 @@
         ends = []
         for jj in range(NJ):
             j = k * NJ + jj
-            picked = jnp.concatenate([tok[rows[s, j]] for s in range(CAP)], 1)
+            picked = jnp.concatenate([tok[table[s, j]] for s in range(CAP)], 1)
             weight = sv[pl.ds(0, CAP), :, columns(j)].reshape(CAP * BLK, BLK)
             result = jnp.dot(picked, weight, preferred_element_type=F32)
             for d in range(R):
@@ -372,7 +378,7 @@
         terms = []
         for jj in range(NJ):
             j = k * NJ + jj
-            picked = jnp.concatenate([tokt[rows[s, j]] for s in range(CAP)], 0)
+            picked = jnp.concatenate([tokt[table[s, j]] for s in range(CAP)], 0)
             grad = jnp.concatenate([blocks[jj], jnp.zeros((2 * BLK - TOK, BLK), BF16)], 0)
             term = jnp.dot(picked, grad, preferred_element_type=F32)
             terms.append(term.astype(BF16).reshape(Y, X, 16, BLK))
@@ -399,7 +405,7 @@
         def pair(p, carry):
             weights = [
                 jnp.concatenate(
-                    [sv[inv[2 * p + i, k * NJ + jj], :, columns(k * NJ + jj)] for jj in range(NJ)],
+                    [sv[table[CAP + 2 * p + i, k * NJ + jj], :, columns(k * NJ + jj)] for jj in range(NJ)],
                     1,
                 )
                 for i in range(2)
@@ -464,71 +470,67 @@
         for jj in range(NJ):
             sg_out[:, columns(k * NJ + jj)] = total[jj] * factor
 
-    def sums_2(k):
-        by_path(k, lambda: ring_ax.advance(k, 2), lambda: ring_by.advance(k, 2))
-
-    def sums_3(k):
-        def x_first():
-            ya[k] = ring_ax.finish(k).astype(BF16)
-            direct_ay.start(k)
-
-        by_path(k, x_first, lambda: ring_by.advance(k, 3))
-
-    def sums_4(k):
-        def x_first():
-            write(k, direct_ay.finish(k))
-            direct_ay.drain(k)
-
-        by_path(k, x_first, lambda: ring_by.advance(k, 4))
-
-    def sums_5(k):
-        def y_first():
-            xb[k] = ring_by.finish(k).astype(BF16)
-            direct_bx.start(k)
-
-        by_path(k, lambda: None, y_first)
-
-    def sums_6(k):
-        def y_first():
-            write(k, direct_bx.finish(k))
-            direct_bx.drain(k)
-
-        by_path(k, lambda: None, y_first)
-
+    def x_last(k):
+        ya[k] = ring_ax.finish(k).astype(BF16)
+        direct_ay.start(k)
+
+    def x_first_sum(k):
+        write(k, direct_ay.finish(k))
+        direct_ay.drain(k)
+
+    def y_last(k):
+        xb[k] = ring_by.finish(k).astype(BF16)
+        direct_bx.start(k)
+
+    def y_first_sum(k):
+        write(k, direct_bx.finish(k))
+        direct_bx.drain(k)
+
+    def only_x(work):
+        return lambda k: by_path(k, lambda: work(k), lambda: None)
+
+    def only_y(work):
+        return lambda k: by_path(k, lambda: None, lambda: work(k))
+
+    ready = 6 * LAG
     stages = (
-        (6, lambda k: gather(k, 3)),
-        (5, lambda k: gather(k, 2)),
-        (4, lambda k: gather(k, 1)),
-        (3, activate),
-        (2, lambda k: row_sum(k, 3)),
-        (1, lambda k: row_sum(k, 2)),
-        (11, sums_6),
-        (10, sums_5),
-        (9, sums_4),
-        (8, sums_3),
-        (7, sums_2),
-        (6, weight_grad),
+        (5 * LAG, lambda k: gather(k, 2)),
+        (4 * LAG, lambda k: gather(k, 1)),
+        (3 * LAG, activate),
+        (2 * LAG, lambda k: row_sum(k, 3)),
+        (LAG, lambda k: row_sum(k, 2)),
+        (ready + X_FIRST[0], only_x(lambda k: ring_ax.advance(k, 2))),
+        (ready + Y_FIRST[2], only_y(lambda k: ring_by.advance(k, 4))),
+        (ready + Y_FIRST[1], only_y(lambda k: ring_by.advance(k, 3))),
+        (ready + Y_FIRST[0], only_y(lambda k: ring_by.advance(k, 2))),
+        (ready + X_FIRST[1], only_x(x_last)),
+        (ready + Y_FIRST[3], only_y(y_last)),
+        (ready, lambda k: gather(k, 3)),
+        (ready, weight_grad),
         (0, forward),
-        (6, token_grad),
+        (ready, token_grad),
+        (ready + X_FIRST[2], only_x(x_first_sum)),
+        (ready + Y_FIRST[4], only_y(y_first_sum)),
     )
 
     def tick(t, carry):
         for stage, work in stages:
-            k = t - stage * LAG
+            k = t - stage
 
             @pl.when((k >= 0) & (k < NC))
             def _():
                 work(k)
 
-        for stage, work in ((6, tg_first), (7, tg_second)):
-
-            @pl.when(t == NC - 1 + stage * LAG)
+        for stage, work in ((ready, tg_first), (ready + X_FIRST[0], tg_second)):
+
+            @pl.when(t == NC - 1 + stage)
             def _():
                 work()
 
         return carry
 
-    lax.fori_loop(0, max(NC + 9 * LAG, 5 + 11 * LAG), tick, 0)
+    ticks = max(NC + ready + X_FIRST[2], Y_CHUNKS[-1] + 1 + ready + Y_FIRST[4])
+    lax.fori_loop(0, ticks, tick, 0)
     tg_last()
 
 
@@ -537,6 +539,7 @@
     slots = jnp.arange(CAP, dtype=jnp.int32)
     match = slot_rows[None, :, :] == blocks[:, None, None]
     inverse = jnp.min(jnp.where(match, slots[None, :, None], CAP), axis=1)
+    table = jnp.concatenate([slot_rows, inverse], axis=0)
 
     def dma(*shape):
         return pltpu.SemaphoreType.DMA(shape)
@@ -554,7 +557,7 @@
             jax.ShapeDtypeStruct((18, 16, BLK), BF16),
             jax.ShapeDtypeStruct((16, COLS * BLK), F32),
         ),
-        in_specs=[vmem, smem, smem, vmem, pl.BlockSpec(memory_space=pl.ANY)],
+        in_specs=[vmem, smem, vmem, pl.BlockSpec(memory_space=pl.ANY)],
         out_specs=(vmem, vmem, vmem),
         scratch_shapes=[
             buf(2 * Z, 18, 16, BLK),
@@ -584,9 +587,9 @@
             pltpu.SemaphoreType.DMA,
             dma(2, 5),
             dma(2, 2 * Z),
-            dma(2, R + 6),
+            dma(SLOTS, R + 6),
             dma(NC, 3 * R),
-            dma(2, 22),
+            dma(SLOTS, 22),
             dma(NC, 22),
             dma(3),
             dma(3),
@@ -594,7 +597,7 @@
         compiler_params=pltpu.CompilerParams(
             collective_id=0, has_side_effects=True, vmem_limit_bytes=52 * 1024 * 1024
         ),
-    )(tokens_in, slot_rows, inverse, act_cotangent, slot_values.reshape(CAP, BLK, COLS * BLK))
+    )(tokens_in, table, act_cotangent, slot_values.reshape(CAP, BLK, COLS * BLK))
 
     mains = packed[:, : 2 * NJ].reshape(NC, NJ, 32, BLK)
     ends = packed[:, 2 * NJ].reshape(NC, NJ, 4, BLK)

time: 106 us -> 102 us (0.962)
  Pallas kernels: 99.4 us -> 94.9 us
    pallas_call x1, Pallas kernels: 99.4 us -> 94.9 us  [body(): pl.pallas_call(kernel, out_shape=(jax.ShapeDtypeStruct((NC, tiles, 16, BL...]
    unnamed x7 -> x5, local copies, waits for them, and re-layouts: 3.5 us -> 2.83 us
where the time goes in v3:
time: 102 us
  Pallas kernels  94.9 us (93%)
  local copies, waits for them, and re-layouts  4.59 us (4%)
  other arithmetic  1.44 us (1%)
    pallas_call x1, Pallas kernels, body(): pl.pallas_call(kernel, out_shape=(jax.ShapeDtypeStruct((NC, tiles, 16, BL...  94.9 us
    unnamed x5, local copies, waits for them, and re-layouts  2.83 us

profile of v3, /device:TPU:8, one launch (start us, length us, event | category | flops | bytes accessed | tf_op | source)
XLA Modules:
  0.0 101.6 jit_solution(4560174352040770361)
XLA Ops:
  0.6 0.7 select_reduce_fusion
  1.3 0.7 pad_add_fusion.table
  2.0 0.0 copy-start
  2.0 1.0 copy-done
  3.0 0.0 copy-start.1
  3.0 0.9 copy-done.1
  3.9 94.9 %shard_map.67 = (bf16[8,9,16,128]{3,2,1,0:T(8,128)(2,1)S(1)}, bf16[18,16,128]{2,1,0:T(8,128)(2,1)S(1)}, f32[16,4096]{1,0:T(8,128)S(1)}) custom-call(bf16[24,1536]{1,0:T(8,128)(2,1)S(1)} %copy-done.1, s32[16,32]{1,0:T(8,128)S(1)} %pad_add_fusion.table, bf16[36,4096]{1,0:T(8,128)(2,1)S(1)} %copy-done, bf16[4,128,4096]{2,1,0:T(8,128)(2,1)} %bitcast.11), custom_call_target="tpu_custom_call" | custom-call | tf_op jit(solution)/shard_map/pallas_call | solution.py:553
  98.9 0.1 copy.11
  98.9 0.7 reshape.29
  99.6 1.0 copy.12
  100.6 0.1 copy.10
  100.7 0.9 reshape.27
  (3 shorter events, 0.1 us)
Async XLA Ops:
  2.0 1.0 copy-start
  3.0 0.9 copy-start.1

commit v4 on v3

--- a/solution.py
+++ b/solution.py
@@ -460,7 +460,9 @@
         tg_copy(1).wait_recv()
         tg_copy(2).wait_recv()
         total = tgs[core, z].astype(F32) + tgr2[0].astype(F32) + tgr2[1].astype(F32)
-        tg_out[...] = total.astype(BF16)
+        total = total.reshape(BT // 2, 48, BLK)
+        for b in range(BT):
+            tg_out[:, b * BLK : (b + 1) * BLK] = total[b // 2, 24 * (b % 2) : 24 * (b % 2) + 24].astype(BF16)
         tg_copy(1).wait_send()
         tg_copy(2).wait_send()
 
@@ -494,11 +496,12 @@
 
     ready = 6 * LAG
     stages = (
+        (0, forward),
+        (LAG, lambda k: row_sum(k, 2)),
+        (2 * LAG, lambda k: row_sum(k, 3)),
+        (3 * LAG, activate),
+        (4 * LAG, lambda k: gather(k, 1)),
         (5 * LAG, lambda k: gather(k, 2)),
-        (4 * LAG, lambda k: gather(k, 1)),
-        (3 * LAG, activate),
-        (2 * LAG, lambda k: row_sum(k, 3)),
-        (LAG, lambda k: row_sum(k, 2)),
         (ready + X_FIRST[0], only_x(lambda k: ring_ax.advance(k, 2))),
         (ready + Y_FIRST[2], only_y(lambda k: ring_by.advance(k, 4))),
         (ready + Y_FIRST[1], only_y(lambda k: ring_by.advance(k, 3))),
@@ -507,7 +510,6 @@
         (ready + Y_FIRST[3], only_y(y_last)),
         (ready, lambda k: gather(k, 3)),
         (ready, weight_grad),
-        (0, forward),
         (ready, token_grad),
         (ready + X_FIRST[2], only_x(x_first_sum)),
         (ready + Y_FIRST[4], only_y(y_first_sum)),
@@ -550,11 +552,11 @@
     vmem = pl.BlockSpec(memory_space=pltpu.VMEM)
     smem = pl.BlockSpec(memory_space=pltpu.SMEM)
     tiles = 2 * NJ + 1
-    packed, grad, summed = pl.pallas_call(
+    packed, token_grad, summed = pl.pallas_call(
         kernel,
         out_shape=(
             jax.ShapeDtypeStruct((NC, tiles, 16, BLK), BF16),
-            jax.ShapeDtypeStruct((18, 16, BLK), BF16),
+            jax.ShapeDtypeStruct((24, BT * BLK), BF16),
             jax.ShapeDtypeStruct((16, COLS * BLK), F32),
         ),
         in_specs=[vmem, smem, vmem, pl.BlockSpec(memory_space=pl.ANY)],
@@ -602,7 +604,6 @@
     mains = packed[:, : 2 * NJ].reshape(NC, NJ, 32, BLK)
     ends = packed[:, 2 * NJ].reshape(NC, NJ, 4, BLK)
     activation = jnp.concatenate([mains, ends], axis=2).transpose(2, 0, 1, 3).reshape(36, COLS * BLK)
-    token_grad = grad.reshape(BT // 2, 2, 24, BLK).transpose(2, 0, 1, 3).reshape(24, BT * BLK)
     slot_grad = summed.reshape(16, 1, COLS * BLK)
     return (activation, token_grad, slot_grad)
 

time: 102 us -> 100 us (0.980)
  the two profiles are of different devices: /device:TPU:8 before, /device:TPU:2 now
where the time goes in v4:
time: 100 us; the launch traced here: 99.8 us
  Pallas kernels  93.2 us (93%)
  local copies, waits for them, and re-layouts  4.5 us (4%)
  other arithmetic  1.44 us (1%)
    pallas_call x1, Pallas kernels, body(): pl.pallas_call(kernel, out_shape=(jax.ShapeDtypeStruct((NC, tiles, 16, BL...  93.2 us
    unnamed x6, local copies, waits for them, and re-layouts  3.46 us

profile of v4, /device:TPU:2, one launch (start us, length us, event | category | flops | bytes accessed | tf_op | source)
XLA Modules:
  0.0 99.8 jit_solution(13503533845155926619)
XLA Ops:
  0.6 0.7 select_reduce_fusion
  1.3 0.7 pad_add_fusion.table
  2.0 0.0 copy-start
  2.0 1.0 copy-done
  3.0 0.0 copy-start.1
  3.0 0.9 copy-done.1
  3.9 93.2 %shard_map.67 = (bf16[8,9,16,128]{3,2,1,0:T(8,128)(2,1)S(1)}, bf16[24,1536]{1,0:T(8,128)(2,1)S(1)}, f32[16,4096]{1,0:T(8,128)S(1)}) custom-call(bf16[24,1536]{1,0:T(8,128)(2,1)S(1)} %copy-done.1, s32[16,32]{1,0:T(8,128)S(1)} %pad_add_fusion.table, bf16[36,4096]{1,0:T(8,128)(2,1)S(1)} %copy-done, bf16[4,128,4096]{2,1,0:T(8,128)(2,1)} %bitcast.7), custom_call_target="tpu_custom_call" | custom-call | tf_op jit(solution)/shard_map/pallas_call | solution.py:555
  97.1 1.0 copy.10
  98.1 0.1 copy.9
  98.2 0.9 reshape.21
  99.1 0.6 copy.12
  (3 shorter events, 0.1 us)
Async XLA Ops:
  2.0 1.0 copy-start
  3.0 0.9 copy-start.1

commit v5 on v4

--- a/solution.py
+++ b/solution.py
@@ -361,7 +361,9 @@
         value, slope = gelu_pair(hidden)
         hg[k, row] = (cot[k].astype(F32) * slope).astype(BF16)
         gather(k, 0)
-        act_out[k] = value.astype(BF16)
+        for jj in range(NJ):
+            act_out[pl.ds(0, 32), columns(k * NJ + jj)] = value[2 * jj : 2 * jj + 2].reshape(32, BLK).astype(BF16)
+            act_out[pl.ds(32, 4), columns(k * NJ + jj)] = value[2 * NJ, 4 * jj : 4 * jj + 4].astype(BF16)
         row_sum_drain(k, R - 1)
 
     def grad_blocks(k):
@@ -552,10 +554,10 @@
     vmem = pl.BlockSpec(memory_space=pltpu.VMEM)
     smem = pl.BlockSpec(memory_space=pltpu.SMEM)
     tiles = 2 * NJ + 1
-    packed, token_grad, summed = pl.pallas_call(
+    activation, token_grad, summed = pl.pallas_call(
         kernel,
         out_shape=(
-            jax.ShapeDtypeStruct((NC, tiles, 16, BLK), BF16),
+            jax.ShapeDtypeStruct((36, COLS * BLK), BF16),
             jax.ShapeDtypeStruct((24, BT * BLK), BF16),
             jax.ShapeDtypeStruct((16, COLS * BLK), F32),
         ),
@@ -601,9 +603,6 @@
         ),
     )(tokens_in, table, act_cotangent, slot_values.reshape(CAP, BLK, COLS * BLK))
 
-    mains = packed[:, : 2 * NJ].reshape(NC, NJ, 32, BLK)
-    ends = packed[:, 2 * NJ].reshape(NC, NJ, 4, BLK)
-    activation = jnp.concatenate([mains, ends], axis=2).transpose(2, 0, 1, 3).reshape(36, COLS * BLK)
     slot_grad = summed.reshape(16, 1, COLS * BLK)
     return (activation, token_grad, slot_grad)
 

time: 100 us -> 99.7 us (level)
    unnamed x6 -> x7, local copies, waits for them, and re-layouts: 3.46 us -> 4.18 us
where the time goes in v5:
time: 99.7 us; the launch traced here: 99.4 us
  Pallas kernels  93.2 us (93%)
  local copies, waits for them, and re-layouts  4.18 us (4%)
  other arithmetic  1.4 us (1%)
    pallas_call x1, Pallas kernels, body(): pl.pallas_call(kernel, out_shape=(jax.ShapeDtypeStruct((36, COLS * BLK),...  93.2 us
    unnamed x7, local copies, waits for them, and re-layouts  4.18 us

profile of v5, /device:TPU:2, one launch (start us, length us, event | category | flops | bytes accessed | tf_op | source)
XLA Modules:
  0.0 99.4 jit_solution(6132435767621447554)
XLA Ops:
  0.6 0.7 select_reduce_fusion
  1.3 0.7 pad_add_fusion.table
  2.0 0.0 copy-start
  2.0 1.0 copy-done
  3.0 0.0 copy-start.1
  3.0 0.9 copy-done.1
  3.9 93.2 %shard_map.67 = (bf16[36,4096]{1,0:T(8,128)(2,1)S(1)}, bf16[24,1536]{1,0:T(8,128)(2,1)S(1)}, f32[16,4096]{1,0:T(8,128)S(1)}) custom-call(bf16[24,1536]{1,0:T(8,128)(2,1)S(1)} %copy-done.1, s32[16,32]{1,0:T(8,128)S(1)} %pad_add_fusion.table, bf16[36,4096]{1,0:T(8,128)(2,1)S(1)} %copy-done, bf16[4,128,4096]{2,1,0:T(8,128)(2,1)} %bitcast.3), custom_call_target="tpu_custom_call" | custom-call | tf_op jit(solution)/shard_map/pallas_call | solution.py:557
  97.1 1.0 copy.8
  98.0 0.7 copy.11
  98.8 0.6 copy.12
Async XLA Ops:
  2.0 1.0 copy-start
  3.0 0.9 copy-start.1
